TPU v7x, 256 devices: a whole 4x4x8 slice. The times are simulated.
256 devices in a mesh: ctx: 16 (over y, x), tp: 16 (over z, core).
Axes of the slice: x: 4, y: 4, z: 8, core: 2. Of those that a mesh axis runs over, the one named last changes fastest.
Arguments:
- inner_act: bfloat16 [4096, 16384], P('ctx', 'tp'), may hold values from -6 to 6
- step_sizes: float32 [4096, 128], P('ctx', 'tp'), may hold values from 0.3 to 3
- in_coupling: bfloat16 [4096, 8, 128], P('ctx'), may hold values from -0.59765625 to 0.59765625
- out_coupling: bfloat16 [4096, 8, 128], P('ctx'), may hold values from -0.59765625 to 0.59765625
- log_rates: float32 [128], P('tp'), may hold values from -11.5 to -3.5
- skip_gain: float32 [128], P('tp'), may hold values from 0.5 to 2
- state_init: float32 [128, 128, 128], P('tp'), may hold values from -6 to 6
- out_weight: bfloat16 [16384, 8192], P('tp', 'ctx'), may hold values from -0.046875 to 0.046875
- cotangent: bfloat16 [4096, 8192], P('tp', 'ctx'), may hold values from -6 to 6
Outputs:
- mixed: bfloat16 [4096, 8192], P('tp', 'ctx')
- grad_inner: bfloat16 [4096, 16384], P('ctx', 'tp')
- grad_weight: bfloat16 [16384, 8192], P('tp', 'ctx')
- grad_state: float32 [128, 128, 128], P('tp', 'ctx')
All inputs are finite; a program needn't handle non-finite values.
Results may differ from a plain program's by a relative error of at most 0.0049.
Values may be sent and summed in bfloat16 or wider, within the bound.
A program may use at most 128 MiB of HBM per device.

v0:
```python
import jax
import jax.numpy as jnp
from jax import lax
from jax.sharding import PartitionSpec as P

highest = lax.Precision.HIGHEST


def carried_in(shard, axis, combine, identity, reverse):
    count, place = (lax.axis_size(axis), lax.axis_index(axis))
    everything = jax.tree.map(lambda part: lax.all_gather(part, axis), shard)
    start = jax.tree.map(
        lambda part, zero: jnp.broadcast_to(jnp.asarray(zero, part.dtype), part.shape),
        shard,
        identity,
    )

    def hop(k, before):
        at = count - 1 - k if reverse else k
        reached = at > place if reverse else at < place
        new = combine(before, jax.tree.map(lambda part: part[at], everything))
        return jax.tree.map(lambda a, b: jnp.where(reached, a, b), new, before)

    return lax.fori_loop(0, count, hop, start)


def block_terms(step_block, write_block, read_block, rates):
    cumlog = jnp.cumsum(-step_block * rates[None, :], axis=0)
    length = cumlog.shape[0]
    causal = jnp.arange(length)[:, None] >= jnp.arange(length)[None, :]
    spread = cumlog.T[:, :, None] - cumlog.T[:, None, :]
    decays = jnp.where(causal[None], jnp.exp(jnp.where(causal[None], spread, 0.0)), 0.0)
    scores = jnp.einsum("thn,shn->hts", read_block, write_block, precision=highest) * decays
    trailing = jnp.exp(cumlog[-1][None, :] - cumlog)
    return (cumlog, scores, trailing)


def local_state(terms, values, step_block, write_block):
    cumlog, scores, trailing = terms
    inputs = step_block[:, :, None] * values
    own_state = jnp.einsum("sh,shp,shn->hpn", trailing, inputs, write_block, precision=highest)
    return (jnp.exp(cumlog[-1]), own_state)


def block_output(terms, values, step_block, read_block, skip_gain, state_in):
    cumlog, scores, trailing = terms
    inputs = step_block[:, :, None] * values
    inner = jnp.einsum("hts,shp->thp", scores, inputs, precision=highest)
    carried = jnp.exp(cumlog)[:, :, None] * jnp.einsum(
        "thn,hpn->thp", read_block, state_in, precision=highest
    )
    return inner + carried + skip_gain[None, :, None] * values


def block_reach(terms, grad_block, read_block):
    cumlog, scores, trailing = terms
    return jnp.einsum("th,thp,thn->hpn", jnp.exp(cumlog), grad_block, read_block, precision=highest)


def block_grad_x(terms, grad_block, step_block, write_block, skip_gain, state_after):
    cumlog, scores, trailing = terms
    grad_in = jnp.einsum("hts,thp->shp", scores, grad_block, precision=highest)
    grad_in = grad_in + trailing[:, :, None] * jnp.einsum(
        "hpn,shn->shp", state_after, write_block, precision=highest
    )
    return step_block[:, :, None] * grad_in + skip_gain[None, :, None] * grad_block


def combine(earlier, later):
    return (earlier[0] * later[0], later[0][:, None, None] * earlier[1] + later[1])


def local(
    inner_act,
    step_sizes,
    in_coupling,
    out_coupling,
    log_rates,
    skip_gain,
    state_init,
    out_weight,
    cotangent,
):
    length = inner_act.shape[0]
    heads_dev = step_sizes.shape[1]
    head_size = state_init.shape[1]
    state_size = state_init.shape[2]
    groups = in_coupling.shape[1]
    total_heads = heads_dev * lax.axis_size("tp")
    rates = jnp.exp(log_rates)
    values = inner_act.astype(jnp.float32).reshape(length, heads_dev, head_size)
    group_of = (lax.axis_index("tp") * heads_dev + jnp.arange(heads_dev)) // (total_heads // groups)
    chooser = (group_of[:, None] == jnp.arange(groups)[None, :]).astype(jnp.float32)
    write_block = jnp.einsum(
        "lgn,hg->lhn", in_coupling.astype(jnp.float32), chooser, precision=highest
    )
    read_block = jnp.einsum(
        "lgn,hg->lhn", out_coupling.astype(jnp.float32), chooser, precision=highest
    )
    terms = block_terms(step_sizes, write_block, read_block, rates)
    block_decay, own_state = local_state(terms, values, step_sizes, write_block)
    identity = (
        jnp.ones((heads_dev,), jnp.float32),
        jnp.zeros((heads_dev, head_size, state_size), jnp.float32),
    )
    before_decay, before_state = carried_in(
        (block_decay, own_state), "ctx", combine, identity, False
    )
    state_in = before_state + before_decay[:, None, None] * state_init
    mixer_out = block_output(terms, values, step_sizes, read_block, skip_gain, state_in)
    mixer_out = mixer_out.reshape(length, heads_dev * head_size).astype(jnp.bfloat16)
    mixer_all = lax.all_gather(mixer_out, "ctx", axis=0, tiled=True)
    mixed = lax.psum_scatter(
        jnp.dot(mixer_all, out_weight, preferred_element_type=jnp.float32),
        "tp",
        scatter_dimension=0,
        tiled=True,
    ).astype(jnp.bfloat16)
    cot_all = lax.all_gather(cotangent, "tp", axis=0, tiled=True)
    grad_weight = lax.dot_general(
        mixer_all, cot_all, (((0,), (0,)), ((), ())), preferred_element_type=jnp.float32
    ).astype(jnp.bfloat16)
    cot_own = lax.all_to_all(cot_all, "ctx", split_axis=0, concat_axis=1, tiled=True)
    grad_mixer = lax.dot_general(
        cot_own,
        lax.all_gather(out_weight, "ctx", axis=1, tiled=True),
        (((1,), (1,)), ((), ())),
        preferred_element_type=jnp.float32,
    )
    grad_block = grad_mixer.reshape(length, heads_dev, head_size)
    reach = block_reach(terms, grad_block, read_block)
    after_decay, after_state = carried_in((block_decay, reach), "ctx", combine, identity, True)
    grad_x = block_grad_x(terms, grad_block, step_sizes, write_block, skip_gain, after_state)
    grad_inner = grad_x.reshape(length, heads_dev * head_size).astype(jnp.bfloat16)
    init_term = before_decay[:, None, None] * reach
    grad_state = lax.psum_scatter(init_term, "ctx", scatter_dimension=1, tiled=True)
    return (mixed, grad_inner, grad_weight, grad_state)


def solution(mesh):
    placed = (
        P("ctx", "tp"),
        P("ctx", "tp"),
        P("ctx", None, None),
        P("ctx", None, None),
        P("tp"),
        P("tp"),
        P("tp", None, None),
        P("tp", "ctx"),
        P("tp", "ctx"),
    )
    return jax.shard_map(
        local,
        mesh=mesh,
        in_specs=placed,
        out_specs=(P("tp", "ctx"), P("ctx", "tp"), P("tp", "ctx"), P("tp", "ctx", None)),
        check_vma=False,
    )
```

profile of v0, /device:TPU:2, one launch (start us, length us, event | category | flops | bytes accessed | tf_op | source)
XLA Modules:
  0.0 620.0 jit_solution(11613525414366784233)
XLA Ops:
  9.9 1.3 copy.53
  11.5 2.8 fusion.13
  15.9 20.6 %all-gather.2 = f32[16,1,8]{2,1,0:T(1,128)S(1)} all-gather(f32[1,1,8]{2,1,0:T(1,128)S(1)} %bitcast.98), channel_id=1, replica_groups=mesh['ctx'=16,'tp'=16] {'ctx'}, dimensions={0}, use_global_device_ids=true | all-gather | bytes 544 | tf_op jit(solution)/shard_map/all_gather | solution.py:11
  38.0 3.7 select_multiply_fusion
  41.6 51.7 %all-gather.15.cloned.1.call-done = f32[128,128,128]{2,1,0:T(8,128)} async-done(((f32[8,128,128]{2,1,0:T(8,128)}), f32[128,128,128]{2,1,0:T(8,128)}) %all-gather.15.cloned.1.call-update) | async-done | bytes 8388624 | tf_op jit(solution)/shard_map/all_gather | solution.py:11
  93.3 19.6 %while.32 = (s32[]{:T(128)}, f32[8]{0:T(128)S(1)}, f32[8,128,128]{2,1,0:T(8,128)S(1)}, s32[]{:T(128)}, f32[16,8]{1,0:T(8,128)S(1)}, /*index=5*/f32[16,8,128,128]{3,2,1,0:T(8,128)}, s32[]{:T(128)}, s32[]{:T(128)}) while((s32[]{:T(128)}, f32[8]{0:T(128)S(1)}, f32[8,128,128]{2,1,0:T(8,128)S(1)}, s32[]{:T(128)}, ...), condition=%wide.region_3.4_spmd.clone, body=%wide.region_2.3_spmd.clone.sunk | while | flops 524316 | bytes 1573147 | solution.py:24
  112.9 2.6 fusion.8
  115.5 3.1 fusion.10
  118.6 18.4 %all-gather.11.cloned.1.call-done = bf16[4096,512]{1,0:T(8,128)(2,1)} async-done(((bf16[256,512]{1,0:T(8,128)(2,1)}), bf16[4096,512]{1,0:T(8,128)(2,1)}) %all-gather.11.cloned.1.call-update) | async-done | bytes 4194320 | tf_op jit(solution)/shard_map/all_gather | solution.py:119
  137.1 74.0 %all_to_all.19 = bf16[16,256,512]{2,1,0:T(8,128)(2,1)S(1)} all-to-all(bf16[16,256,512]{2,1,0:T(8,128)(2,1)} %bitcast.92), channel_id=1, replica_groups=mesh['ctx'=16,'tp'=16] {'ctx'}, dimensions={0} | all-to-all | bytes 8388608 | tf_op jit(solution)/shard_map/all_to_all | solution.py:123
  211.1 4.5 copy.60
  215.5 7.4 %reshape.104 = bf16[256,8192,1]{1,0,2:T(8,128)(2,1)} reshape(bf16[256,16,512]{2,1,0:T(8,128)(2,1)} %copy.60) | data formatting | bytes 8388608 | tf_op jit(solution)/shard_map/all_to_all | solution.py:123
  223.0 74.1 %all-gather.13.cloned.1.call-done = bf16[1024,8192]{1,0:T(8,128)(2,1)} async-done(((bf16[1024,512]{1,0:T(8,128)(2,1)}), bf16[1024,8192]{1,0:T(8,128)(2,1)}) %all-gather.13.cloned.1.call-update) | async-done | bytes 16777232 | tf_op jit(solution)/shard_map/all_gather | solution.py:126
  297.1 9.4 %fusion.37 = f32[256,8,128]{0,2,1:T(8,128)S(1)} fusion(bf16[256,8192,1]{1,0,2:T(8,128)(2,1)} %reshape.104, bf16[8,128,8192]{2,1,0:T(8,128)(2,1)} %bitcast.99), kind=kOutput, calls=%fused_computation.63 | convolution fusion | flops 4294967296 | bytes 22020096 | tf_op jit(solution)/shard_map/dot_general | solution.py:124
  306.5 2.3 broadcast_multiply_fusion
  308.9 73.9 %all-gather.9.cloned.1.call-done = bf16[4096,1024]{0,1:T(8,128)(2,1)} async-done(((bf16[256,1024]{0,1:T(8,128)(2,1)}), bf16[4096,1024]{0,1:T(8,128)(2,1)}) %all-gather.9.cloned.1.call-update) | async-done | bytes 8388624 | tf_op jit(solution)/shard_map/all_gather | solution.py:112
  382.7 11.4 %fusion.36 = f32[4096,512]{1,0:T(8,128)} fusion(bf16[4096,1024]{0,1:T(8,128)(2,1)} %all-gather.9.cloned.1.call-done, bf16[1024,512]{1,0:T(8,128)(2,1)} %param.20), kind=kOutput, calls=%fused_computation.62 | convolution fusion | flops 4294967296 | bytes 17825792 | tf_op jit(solution)/shard_map/dot_general | solution.py:114
  394.9 10.6 %convolution_convert_fusion = bf16[1024,512]{1,0:T(8,128)(2,1)} fusion(bf16[4096,1024]{0,1:T(8,128)(2,1)} %all-gather.9.cloned.1.call-done, bf16[4096,512]{1,0:T(8,128)(2,1)} %all-gather.11.cloned.1.call-done), kind=kOutput, calls=%fused_computation.9 | convolution fusion | flops 4295491584 | bytes 13631488 | tf_op jit(solution)/shard_map/dot_general | solution.py:120
  405.5 55.1 %all-gather.17.cloned.1.call-done = f32[128,128,128]{2,1,0:T(8,128)} async-done(((f32[8,128,128]{2,1,0:T(8,128)}), f32[128,128,128]{2,1,0:T(8,128)}) %all-gather.17.cloned.1.call-update) | async-done | bytes 8388624 | tf_op jit(solution)/shard_map/all_gather | solution.py:11
  460.6 19.6 %while.33 = (s32[]{:T(128)}, f32[8,128,128]{2,1,0:T(8,128)S(1)}, s32[]{:T(128)}, f32[16,8]{1,0:T(8,128)S(1)}, f32[16,8,128,128]{3,2,1,0:T(8,128)}, /*index=5*/s32[]{:T(128)}, s32[]{:T(128)}, s32[]{:T(128)}, s32[]{:T(128)}) while((s32[]{:T(128)}, f32[8,128,128]{2,1,0:T(8,128)S(1)}, s32[]{:T(128)}, f32[16,8]{1,0:T(8,128)S(1)}, ...), condition=%wide.region_6.7_spmd.clone, body=%wide.region_5.6_spmd.clone.sunk | while | flops 524296 | bytes 1573135 | solution.py:24
  481.4 3.1 fusion.9
  485.5 47.8 %reduce-scatter.3.cloned.1.call-done = f32[256,512]{1,0:T(8,128)} async-done(((f32[4096,512]{1,0:T(8,128)}), f32[256,512]{1,0:T(8,128)}) %reduce-scatter.3.cloned.1.call-update) | async-done | bytes 524304 | tf_op jit(solution)/shard_map/reduce_scatter | solution.py:113
  533.3 1.8 convert_element_type.24
  535.1 78.1 %reduce-scatter.5.cloned.1.call-done = f32[8,8,128]{2,1,0:T(8,128)} async-done(((f32[8,128,128]{2,1,0:T(8,128)}), f32[8,8,128]{2,1,0:T(8,128)}) %reduce-scatter.5.cloned.1.call-update) | async-done | bytes 32784 | tf_op jit(solution)/shard_map/reduce_scatter | solution.py:136
  (115 shorter events, 47.2 us)
Async XLA Ops:
  7.2 4.0 copy-start
  7.2 29.4 %copy-start.5 = (bf16[256,8,128]{2,1,0:T(8,128)(2,1)S(1)}, bf16[256,8,128]{2,1,0:T(8,128)(2,1)}, u32[]{:S(2)}) copy-start(bf16[256,8,128]{2,1,0:T(8,128)(2,1)} %param.16) | copy-start | bytes 1572868
  7.2 86.1 %all-gather.15.cloned.1.call-start = ((), (), s32[]{:S(2)}) async-start(), calls=%async_computation.8 | async-start | bytes 8912896 | tf_op jit(solution)/shard_map/all_gather | solution.py:11
  14.3 122.7 %all-gather.11.cloned.1.call-start = ((), (), s32[]{:S(2)}) async-start(), calls=%async_computation.5 | async-start | bytes 4456448 | tf_op jit(solution)/shard_map/all_gather | solution.py:119
  15.1 282.0 %all-gather.13.cloned.1.call-start = ((), (), s32[]{:S(2)}) async-start(), calls=%async_computation.6 | async-start | bytes 17825792 | tf_op jit(solution)/shard_map/all_gather | solution.py:126
  15.8 366.9 %all-gather.9.cloned.1.call-start = ((), (), s32[]{:S(2)}) async-start(), calls=%async_computation.3 | async-start | bytes 8912896 | tf_op jit(solution)/shard_map/all_gather | solution.py:112
  37.0 1.0 copy-start.2
  41.6 71.3 %copy-start.6 = (f32[8,128,128]{2,1,0:T(8,128)S(1)}, f32[8,128,128]{2,1,0:T(8,128)}, u32[]{:S(2)}) copy-start(f32[8,128,128]{2,1,0:T(8,128)} %param.19) | copy-start | bytes 1572868
  93.3 22.2 %copy-start.7 = (f32[256,8]{0,1:T(8,128)S(1)}, f32[256,8]{0,1:T(8,128)}, u32[]{:S(2)}) copy-start(f32[256,8]{0,1:T(8,128)} %param.14) | copy-start | bytes 24580
  93.3 22.2 %copy-start.8 = (f32[8]{0:T(128)S(1)}, f32[8]{0:T(128)}, u32[]{:S(2)}) copy-start(f32[8]{0:T(128)} %param.18) | copy-start | bytes 100
  112.9 2.6 copy-start.4
  118.6 342.0 %all-gather.17.cloned.1.call-start = ((), (), s32[]{:S(2)}) async-start(), calls=%async_computation.9 | async-start | bytes 8912896 | tf_op jit(solution)/shard_map/all_gather | solution.py:11
  297.1 9.4 %copy-start.3 = (f32[256,8,128]{2,1,0:T(8,128)S(1)}, f32[256,8,128]{2,1,0:T(8,128)}, u32[]{:S(2)}) copy-start(f32[256,8,128]{2,1,0:T(8,128)} %copy-done.2) | copy-start | bytes 3145732
  308.8 224.5 %reduce-scatter.3.cloned.1.call-start = ((), (), s32[]{:S(2)}) async-start(), calls=%async_computation.4 | async-start | bytes 8912896 | tf_op jit(solution)/shard_map/reduce_scatter | solution.py:113
  394.2 219.0 %reduce-scatter.5.cloned.1.call-start = ((), (), s32[]{:S(2)}) async-start(), calls=%async_computation.7 | async-start | bytes 557056 | tf_op jit(solution)/shard_map/reduce_scatter | solution.py:136
  480.1 133.1 %copy-start.1 = (bf16[256,8,128]{2,1,0:T(8,128)(2,1)S(1)}, bf16[256,8,128]{2,1,0:T(8,128)(2,1)}, u32[]{:S(2)}) copy-start(bf16[256,8,128]{2,1,0:T(8,128)(2,1)} %param.15) | copy-start | bytes 1572868
Sparse Core Ops, SparseCore 0:
  14.4 78.7 all-gather.14
  95.1 41.9 all-gather.10
  139.5 157.5 all-gather.12
  299.9 82.7 all-gather.8
  385.0 75.4 all-gather.16
  463.0 70.2 reduce-scatter.2
  537.4 75.8 reduce-scatter.4
where the time goes:
time: 622 us; the launch traced here: 620 us
  waiting for transfers between devices  401 us (64%)
  blocking collectives  94.6 us (15%)
  matrix products  50.8 us (8%)
  other arithmetic  41.4 us (7%)
  local copies, waits for them, and re-layouts  16.4 us (3%)
  between operations  14.3 us (2%)
    all_gather x2, waiting for transfers between devices, carried_in(): everything = jax.tree.map(lambda part: lax.all_gather(part, axis), shard)  107 us
    reduce_scatter x1, waiting for transfers between devices, local(): lax.psum_scatter(init_term, 'ctx', scatter_dimension=1, tiled=True)  78.1 us
    all_gather x1, waiting for transfers between devices, local(): lax.all_gather(out_weight, 'ctx', axis=1, tiled=True)  74.1 us
    all_to_all x1, blocking collectives, local(): lax.all_to_all(cot_all, 'ctx', split_axis=0, concat_axis=1, tiled=True)  74 us
    all_gather x1, waiting for transfers between devices, local(): mixer_all = lax.all_gather(mixer_out, 'ctx', axis=0, tiled=True)  73.9 us
    reduce_scatter x1, waiting for transfers between devices, local(): lax.psum_scatter(jnp.dot(mixer_all, out_weight, preferred_element_type=jn...  47.8 us
    select_n x48, other arithmetic, hop(): return jax.tree.map(lambda a, b: jnp.where(reached, a, b), new, before)  38 us
    all_gather x1, blocking collectives, carried_in(): everything = jax.tree.map(lambda part: lax.all_gather(part, axis), shard)  20.6 us
  transfers between devices with their start and end apart: 7, of which 7 were waited for; matrix products, arithmetic and copies ran while one was open for 16% of the time, Pallas kernels for 0%

commit v1 on v0

v1 whole, which is shorter than its diff:
```python
import jax
import jax.numpy as jnp
from jax import lax
from jax.experimental import pallas as pl
from jax.experimental.pallas import tpu as pltpu
from jax.sharding import PartitionSpec as P

f32 = jnp.float32
bf16 = jnp.bfloat16
L = 256
HD = 8
HH = HD // 2
S = 128
MODEL = 512
HALF = 512
NC = 16
NZ = 8


def mm(a, b):
    return lax.dot_general(a, b, (((1,), (0,)), ((), ())), preferred_element_type=f32)


def mm_bt(a, b):
    return lax.dot_general(a, b, (((1,), (1,)), ((), ())), preferred_element_type=f32)


def mm_at(a, b):
    return lax.dot_general(a, b, (((0,), (0,)), ((), ())), preferred_element_type=f32)


def split(v):
    hi = v.astype(bf16)
    return hi, (v - hi.astype(f32)).astype(bf16)


def rcopy(src, dst, send, recv, device):
    return pltpu.make_async_remote_copy(
        src_ref=src,
        dst_ref=dst,
        send_sem=send,
        recv_sem=recv,
        device_id=device,
        device_id_type=pl.DeviceIdType.MESH,
    )


def kernel(
    lograte_ref, skip_ref, step_ref, x_ref, b_ref, c_ref, init_ref, w_ref, cot_ref,
    mixed_ref, gi_ref, gw_ref, gs_ref,
    cot_all, pa, pb, r1a, r1b, r2a, r2b, r3a, r3b, r4a, r4b, ma, mb,
    own_mix, xs_mix, xr_mix, zs_mix, zr_mix, gw_acc, ybuf, gbuf,
    sb1, rb1, tb1, ub1, sb2, rb2, tb2, ub2,
    stp, cum_s, cumt_s, stept_s, bt_s, ct_s, cb_s,
    z_s, z_r, c_s, c_r, a1s, a1r, a2s, a2r, a3s, a3r, a4s, a4r,
    rsa_s, rsa_r, rsb_s, rsb_r, aga_s, aga_r, agb_s, agb_r, xm_s, xm_r, zm_s, zm_r,
):
    ctx = lax.axis_index("ctx")
    tp = lax.axis_index("tp")
    y, x = ctx // 4, ctx % 4
    z, k = tp // 2, tp % 2
    partner = z * 2 + (1 - k)

    def at_ctx(c):
        return (c, tp)

    def at_z(zz):
        return (ctx, zz * 2 + k)

    def at_y(yy):
        return (yy * 4 + x, tp)

    def at_x(xx):
        return (y * 4 + xx, tp)

    zp, zm = (z + 1) % NZ, (z + 7) % NZ
    other_core = (ctx, partner)

    def wait_in(dst, sem):
        rcopy(dst, dst, sem, sem, other_core).wait_recv()

    def wait_out(src, sem):
        rcopy(src, src, sem, sem, other_core).wait_send()

    barrier = pltpu.get_barrier_semaphore()

    @pl.loop(1, NC)
    def _(i):
        pl.semaphore_signal(
            barrier, inc=1, device_id=at_ctx((ctx + i) % NC), device_id_type=pl.DeviceIdType.MESH
        )

    @pl.loop(1, NZ)
    def _(i):
        pl.semaphore_signal(
            barrier, inc=1, device_id=at_z((z + i) % NZ), device_id_type=pl.DeviceIdType.MESH
        )

    pl.semaphore_signal(
        barrier, inc=1, device_id=other_core, device_id_type=pl.DeviceIdType.MESH
    )

    def zblock(d):
        return ((z + d + NZ) % NZ) * 2 + k

    def pblock(d):
        return ((z + d + NZ) % NZ) * 2 + (1 - k)

    top, bottom = pl.ds(0, L // 2), pl.ds(L // 2, L // 2)
    zcopies = []

    def zsend(src, dst, index, device):
        copy = rcopy(src, dst, z_s.at[index], z_r.at[index], device)
        copy.start()
        zcopies.append(copy)

    def csend(src, dst, index):
        copy = rcopy(src, dst, c_s.at[index], c_r.at[index], other_core)
        copy.start()
        zcopies.append(copy)

    def zstep(step):
        if step == 0:
            zsend(cot_ref, cot_all.at[tp], 0, at_z(zp))
            zsend(cot_ref, cot_all.at[tp], 1, at_z(zm))
            csend(cot_ref, cot_all.at[tp], 0)
            cot_all[tp] = cot_ref[...]
            return
        if step < 4:
            lo, hi = cot_all.at[zblock(-step)], cot_all.at[zblock(step)]
            wait_in(lo, z_r.at[2 * step - 2])
            if step < 3:
                zsend(lo, lo, 2 * step, at_z(zp))
            else:
                part = cot_all.at[zblock(-3), top]
                zsend(part, part, 6, at_z(zp))
            csend(lo, lo, 2 * step - 1)
            wait_in(hi, z_r.at[2 * step - 1])
            if step < 3:
                zsend(hi, hi, 2 * step + 1, at_z(zm))
            else:
                part = cot_all.at[zblock(3), bottom]
                zsend(part, part, 7, at_z(zm))
            csend(hi, hi, 2 * step)
            return
        wait_in(cot_all.at[zblock(4), top], z_r.at[6])
        wait_in(cot_all.at[zblock(4), bottom], z_r.at[7])
        whole = cot_all.at[zblock(4)]
        csend(whole, whole, 7)

    def zpartner(d):
        index = 0 if d == 0 else 7 if d == 4 else 2 * abs(d) - (1 if d < 0 else 0)
        wait_in(cot_all.at[pblock(d)], c_r.at[index])

    lane = lax.broadcasted_iota(jnp.int32, (L, S), 1)
    stp[...] = jnp.zeros_like(stp)
    stp[:, 0:HD] = step_ref[...]
    rate = jnp.exp(lograte_ref[...])
    row_i = lax.broadcasted_iota(jnp.int32, (L, L), 0)
    col_i = lax.broadcasted_iota(jnp.int32, (L, L), 1)
    tri = (row_i >= col_i).astype(f32)
    cum = lax.dot_general(
        tri, -stp[...] * rate, (((1,), (0,)), ((), ())),
        preferred_element_type=f32, precision=lax.Precision.HIGHEST,
    )
    cum_s[...] = cum
    cumt_s[...] = cum.T
    stept_s[...] = stp[...].T
    bt_s[...] = b_ref[...].astype(f32).T
    ct_s[...] = c_ref[...].astype(f32).T

    def col(ref, h):
        return jnp.sum(jnp.where(lane == h, ref[...], 0.0), axis=1, keepdims=True)

    def row(ref, h):
        return ref[pl.ds(h, 1), :]

    def heads(h):
        return pl.ds(pl.multiple_of(h * S, S), S)

    block_decay = jnp.broadcast_to(jnp.exp(cumt_s[0:HD, L - 1 : L]), (HD, S))

    def carry_send(p, sb, rb, ss, rs):
        @pl.loop(1, NC)
        def _(i):
            to = (ctx + i) % NC
            rcopy(
                sb.at[p, to], rb.at[p, ctx], ss.at[p * NC + to], rs.at[p * NC + ctx], at_ctx(to)
            ).start()

        rb[p, ctx] = sb[p, ctx]

    def carry_wait(p, ub, rs):
        @pl.loop(1, NC)
        def _(i):
            at = (ctx + i) % NC
            wait_in(ub.at[p, at], rs.at[p * NC + at])

    def carry_sent(sb, ss):
        for p in range(2):

            @pl.loop(1, NC)
            def _(i):
                to = (ctx + i) % NC
                wait_out(sb.at[p, to], ss.at[p * NC + to])

    def carry_scan(p, rb, tb, first, reverse):
        def hop(i, states):
            at = NC - 1 - i if reverse else i
            out = []
            for h in range(HH):
                tb[p, at, h] = states[h]
                out.append(rb[p, at, HH, h : h + 1, :] * states[h] + rb[p, at, h])
            return tuple(out)

        return lax.fori_loop(0, NC, hop, first)

    def put_piece(sb, p, h, state):
        sb[p, :, h] = state.reshape(NC, HD, S)

    def put_decay(sb, p):
        decay = block_decay[p * HH : (p + 1) * HH, :]
        sb[p, :, HH] = jnp.broadcast_to(jnp.concatenate([decay, decay])[None], (NC, HD, S))

    def own_states(p):
        @pl.loop(0, HH)
        def _(i):
            h = p * HH + i
            a_row = row(cumt_s, h)
            weight = jnp.exp(a_row[:, L - 1 : L] - a_row) * row(stept_s, h)
            hi, lo = split(bt_s[...] * weight)
            xh = x_ref[:, heads(h)]
            put_piece(sb1, p, i, (mm(hi, xh) + mm(lo, xh)).T)

        put_decay(sb1, p)

    def own_outputs(p):
        @pl.loop(p * HH, (p + 1) * HH)
        def _(h):
            a_col = col(cum_s, h)
            a_row = row(cumt_s, h)
            decay = jnp.where(row_i >= col_i, jnp.exp(jnp.minimum(a_col - a_row, 0.0)), 0.0)
            hi, lo = split(cb_s[...] * decay * row(stept_s, h))
            xh = x_ref[:, heads(h)]
            ybuf[:, heads(h)] = mm(hi, xh) + mm(lo, xh) + skip_ref[h] * xh.astype(f32)

    def scan_forward(p):
        carry_wait(p, rb1, a1r)
        first = tuple(
            init_ref[p * HH + i, pl.ds(pl.multiple_of(ctx * HD, HD), HD), :] for i in range(HH)
        )
        carry_scan(p, rb1, tb1, first, False)
        carry_send(p, tb1, ub1, a2s, a2r)

    def finish_outputs(p, m):
        carry_wait(p, ub1, a2r)

        @pl.loop(0, HH)
        def _(i):
            h = p * HH + i
            hi, lo = split(ub1[p, :, i].reshape(S, S))
            carried = jnp.exp(col(cum_s, h)) * (mm_bt(c_ref[...], hi) + mm_bt(c_ref[...], lo))
            m[ctx, :, heads(i)] = (ybuf[:, heads(h)] + carried).astype(bf16)

    own_states(0)
    pl.semaphore_wait(barrier, (NC - 1) + (NZ - 1) + 1)
    carry_send(0, sb1, rb1, a1s, a1r)
    zstep(0)
    own_states(1)
    carry_send(1, sb1, rb1, a1s, a1r)
    cb_s[...] = mm_bt(c_ref[...], b_ref[...])
    own_outputs(0)
    scan_forward(0)
    own_outputs(1)
    scan_forward(1)
    zstep(1)

    def partial_block(j):
        ct = cot_all[j]
        pa[j] = mm_bt(ct, w_ref[0:HALF, :]).astype(bf16)
        pb[j] = mm_bt(ct, w_ref[HALF : 2 * HALF, :]).astype(bf16)

    def partial_pair(d):
        zpartner(d)

        @pl.loop(0, 2)
        def _(i):
            partial_block(((z + d + NZ) % NZ) * 2 + i)

    def ring_sum(part, r1, r2, r3, r4, ss, rs, me1, me2, dev1, dev2, blk, gcol):
        n1p, n1m, far1 = (me1 + 1) % 4, (me1 + 3) % 4, (me1 + 2) % 4
        n2p, n2m = (me2 + 1) % 4, (me2 + 3) % 4
        copies = []

        def q(o):
            return (me2 + o) % 4

        def send(src, dst, index, device):
            copy = rcopy(src, dst, ss.at[index], rs.at[index], device)
            copy.start()
            copies.append(copy)

        plus, minus = (2, 1), (3, 0)

        def step1():
            for i in range(2):
                send(part.at[blk(far1, q(plus[i]))], r1.at[0, i], i, dev1(n1p))
                send(part.at[blk(far1, q(minus[i]))], r1.at[1, i], 2 + i, dev1(n1m))
            for o in minus:
                send(part.at[blk(n1p, q(o))], r2.at[0, o], 4 + o, dev1(n1p))
            for o in plus:
                send(part.at[blk(n1m, q(o))], r2.at[1, o], 8 + o, dev1(n1m))

        def step2():
            for i in range(2):
                for d, (near, order) in enumerate(((n1p, plus), (n1m, minus))):
                    o = order[i]
                    wait_in(r1.at[d, i], rs.at[2 * d + i])
                    j = blk(near, q(o))
                    part[j] = (part[j].astype(f32) + r1[d, i].astype(f32)).astype(bf16)
                    send(part.at[j], r2.at[d, o], 4 + 4 * d + o, dev1(near))

        def total(o):
            wait_in(r2.at[0, o], rs.at[4 + o])
            wait_in(r2.at[1, o], rs.at[8 + o])
            j = blk(me1, q(o))
            return part[j].astype(f32) + r2[0, o].astype(f32) + r2[1, o].astype(f32)

        def step3():
            j = blk(me1, q(2))
            part[j] = total(2).astype(bf16)
            send(part.at[j, top], r3.at[0], 12, dev2(n2p))
            send(part.at[j, bottom], r3.at[1], 13, dev2(n2m))

        def step4():
            for o, near, rows, d in ((1, n2p, top, 0), (3, n2m, bottom, 1)):
                j = blk(me1, q(o))
                part[j] = total(o).astype(bf16)
                wait_in(r3.at[d], rs.at[12 + d])
                part[j, rows] = (part[j, rows].astype(f32) + r3[d].astype(f32)).astype(bf16)
                send(part.at[j], r4.at[d], 14 + d, dev2(near))

        def step5():
            mine = total(0)
            wait_in(r4.at[0], rs.at[14])
            wait_in(r4.at[1], rs.at[15])
            gbuf[:, gcol : gcol + HALF] = mine + r4[0].astype(f32) + r4[1].astype(f32)

        return (step1, step2, step3, step4, step5), copies

    sum_a, copies_a = ring_sum(
        pa, r1a, r2a, r3a, r4a, rsa_s, rsa_r, y, x, at_y, at_x,
        lambda i1, i2: i1 * 4 + i2, 0,
    )
    sum_b, copies_b = ring_sum(
        pb, r1b, r2b, r3b, r4b, rsb_s, rsb_r, x, y, at_x, at_y,
        lambda i1, i2: i2 * 4 + i1, HALF,
    )

    def ring_gather(m, ss, rs, me1, me2, dev1, dev2, blk):
        n1p, n1m, far1 = (me1 + 1) % 4, (me1 + 3) % 4, (me1 + 2) % 4
        n2p, n2m, far2 = (me2 + 1) % 4, (me2 + 3) % 4, (me2 + 2) % 4
        copies = []

        def send(ref, index, device):
            copy = rcopy(ref, ref, ss.at[index], rs.at[index], device)
            copy.start()
            copies.append(copy)

        def at(o):
            return (me1 + o) % 4

        def across(o):
            ref = m.at[blk(at(o), me2)]
            send(ref, 4 + o, dev2(n2p))
            send(ref, 8 + o, dev2(n2m))

        def step1():
            ref = m.at[blk(me1, me2)]
            send(ref, 0, dev1(n1p))
            send(ref, 1, dev1(n1m))
            across(0)

        def step2():
            j = blk(n1m, me2)
            wait_in(m.at[j], rs.at[0])
            send(m.at[j, top], 2, dev1(n1p))
            j = blk(n1p, me2)
            wait_in(m.at[j], rs.at[1])
            send(m.at[j, bottom], 3, dev1(n1m))
            across(3)
            across(1)

        def step3():
            j = blk(far1, me2)
            wait_in(m.at[j, top], rs.at[2])
            wait_in(m.at[j, bottom], rs.at[3])
            across(2)

        def forward(o):
            lo, hi = m.at[blk(at(o), n2m)], m.at[blk(at(o), n2p)]
            wait_in(lo, rs.at[4 + o])
            wait_in(hi, rs.at[8 + o])
            if o in (0, 3):
                send(lo, 12 + o, dev2(n2p))
            else:
                send(hi, 12 + o, dev2(n2m))

        def last(o):
            wait_in(m.at[blk(at(o), far2)], rs.at[12 + o])

        return (step1, step2, step3, forward, last), copies

    gat_a, copies_ga = ring_gather(
        ma, aga_s, aga_r, x, y, at_x, at_y, lambda i1, i2: i2 * 4 + i1
    )
    gat_b, copies_gb = ring_gather(
        mb, agb_s, agb_r, y, x, at_y, at_x, lambda i1, i2: i1 * 4 + i2
    )

    def block_at(ry, rx):
        return ((y + ry) % 4) * 4 + (x + rx) % 4

    def project(j):
        return mm(ma[j], w_ref[0:HALF, :]) + mm(mb[j], w_ref[HALF : 2 * HALF, :])

    def pair(ry, low, high):
        turn = (x + low + k) % 2
        mine = low + turn * (high - low)
        return block_at(ry, mine), block_at(ry, low + high - mine)

    def pair_project(ry, low, high):
        mine, theirs = pair(ry, low, high)
        slot = theirs // 2
        xs_mix[slot] = project(theirs).astype(bf16)
        rcopy(xs_mix.at[slot], xr_mix.at[slot], xm_s.at[slot], xm_r.at[slot], other_core).start()
        own_mix[mine // 2] = project(mine).astype(bf16)

    def pair_send(ry, low, high):
        mine, _ = pair(ry, low, high)
        slot = mine // 2
        wait_in(xr_mix.at[slot], xm_r.at[slot])
        zs_mix[slot] = (own_mix[slot].astype(f32) + xr_mix[slot].astype(f32)).astype(bf16)

        @pl.when(slot != z)
        def _():
            rel = (z - slot + NZ) % NZ
            rcopy(
                zs_mix.at[slot], zr_mix.at[rel], zm_s.at[rel], zm_r.at[rel], (ctx, mine)
            ).start()

    gw_acc[...] = jnp.zeros_like(gw_acc)

    def weight_block(j):
        ct = cot_all[j]
        gw_acc[0:HALF, :] += mm_at(ma[j], ct)
        gw_acc[HALF : 2 * HALF, :] += mm_at(mb[j], ct)

    def pair_weight(ry, low, high):
        weight_block(block_at(ry, low))
        weight_block(block_at(ry, high))

    def own_reach(p):
        @pl.loop(0, HH)
        def _(i):
            h = p * HH + i
            ghi, glo = split(gbuf[:, heads(h)])
            hi, lo = split(ct_s[...] * jnp.exp(row(cumt_s, h)))
            put_piece(sb2, p, i, (mm(hi, ghi) + mm(lo, ghi) + mm(hi, glo)).T)

        put_decay(sb2, p)
        carry_send(p, sb2, rb2, a3s, a3r)

    def own_grads(p):
        @pl.loop(p * HH, (p + 1) * HH)
        def _(h):
            a_col = col(cum_s, h)
            a_row = row(cumt_s, h)
            decay = jnp.where(col_i >= row_i, jnp.exp(jnp.minimum(a_row - a_col, 0.0)), 0.0)
            hi, lo = split(cb_s[...] * decay)
            g = gbuf[:, heads(h)]
            ghi, glo = split(g)
            inner = mm(hi, ghi) + mm(lo, ghi) + mm(hi, glo)
            ybuf[:, heads(h)] = col(stp, h) * inner + skip_ref[h] * g

    def scan_backward(p):
        carry_wait(p, rb2, a3r)
        zero = jnp.zeros((HD, S), f32)
        done = carry_scan(p, rb2, tb2, (zero,) * HH, True)
        for i in range(HH):
            gs_ref[p * HH + i] = done[i]
        carry_send(p, tb2, ub2, a4s, a4r)

    def finish_grads(p):
        carry_wait(p, ub2, a4r)

        @pl.loop(0, HH)
        def _(i):
            h = p * HH + i
            hi, lo = split(ub2[p, :, i].reshape(S, S))
            a_col = col(cum_s, h)
            a_row = row(cumt_s, h)
            trailing = jnp.exp(a_row[:, L - 1 : L] - a_col)
            after = mm_bt(b_ref[...], hi) + mm_bt(b_ref[...], lo)
            total = ybuf[:, heads(h)] + col(stp, h) * trailing * after
            gi_ref[:, heads(h)] = total.astype(bf16)

    early = [(0, 0, 1), (1, 0, 1), (3, 0, 1)]
    late = [(0, 3, 2), (1, 3, 2), (3, 3, 2), (2, 0, 1), (2, 3, 2)]

    finish_outputs(0, ma)
    gat_a[0]()
    finish_outputs(1, mb)
    gat_b[0]()
    partial_pair(0)
    zstep(2)
    gat_a[1]()
    gat_b[1]()
    partial_pair(-1)
    partial_pair(1)
    zstep(3)
    gat_a[2]()
    gat_b[2]()
    partial_pair(-2)
    partial_pair(2)
    zstep(4)
    for o in (0, 3, 1):
        gat_a[3](o)
        gat_b[3](o)
    partial_pair(-3)
    partial_pair(3)
    partial_pair(4)
    gat_a[3](2)
    gat_b[3](2)
    sum_a[0]()
    sum_b[0]()
    for i, p in enumerate(early):
        pair_project(*p)
        if i:
            pair_send(*early[i - 1])
    pair_send(*early[-1])
    for o in (0, 3, 1, 2):
        gat_a[4](o)
        gat_b[4](o)
    for i, p in enumerate(late):
        pair_project(*p)
        if i:
            pair_send(*late[i - 1])
    pair_send(*late[-1])
    sum_a[1]()
    sum_b[1]()
    for p in early + late[:1]:
        pair_weight(*p)
    sum_a[2]()
    sum_b[2]()
    for p in late[1:]:
        pair_weight(*p)
    gw_ref[...] = gw_acc[...].astype(bf16)
    cb_s[...] = mm_bt(b_ref[...], c_ref[...])
    sum_a[3]()
    sum_b[3]()
    sum_a[4]()
    own_reach(0)
    sum_b[4]()
    own_reach(1)
    own_grads(0)
    scan_backward(0)
    own_grads(1)
    scan_backward(1)

    mixed = zs_mix[z].astype(f32)
    for rel in range(1, NZ):
        wait_in(zr_mix.at[rel], zm_r.at[rel])
        mixed = mixed + zr_mix[rel].astype(f32)
    mixed_ref[...] = mixed.astype(bf16)

    finish_grads(0)
    finish_grads(1)

    for copy in zcopies + copies_a + copies_b + copies_ga + copies_gb:
        copy.wait_send()
    carry_sent(sb1, a1s)
    carry_sent(tb1, a2s)
    carry_sent(sb2, a3s)
    carry_sent(tb2, a4s)

    @pl.loop(0, NZ)
    def _(i):
        wait_out(xs_mix.at[i], xm_s.at[i])

    @pl.loop(1, NZ)
    def _(i):
        wait_out(zr_mix.at[i], zm_s.at[i])


def local(inner_act, step_sizes, in_coupling, out_coupling, log_rates, skip_gain, state_init,
          out_weight, cotangent):
    group = lax.axis_index("tp") // 2
    write = lax.dynamic_index_in_dim(in_coupling, group, 1, keepdims=False)
    read = lax.dynamic_index_in_dim(out_coupling, group, 1, keepdims=False)
    rates = jnp.pad(log_rates.reshape(1, HD), ((0, 0), (0, S - HD)))
    vmem = pl.BlockSpec(memory_space=pltpu.VMEM)
    smem = pl.BlockSpec(memory_space=pltpu.SMEM)
    dma = pltpu.SemaphoreType.DMA
    V = pltpu.VMEM
    half = (L, HALF)
    mix = (L, MODEL)
    return pl.pallas_call(
        kernel,
        out_shape=(
            jax.ShapeDtypeStruct((L, MODEL), bf16),
            jax.ShapeDtypeStruct((L, HD * S), bf16),
            jax.ShapeDtypeStruct((HD * S, MODEL), bf16),
            jax.ShapeDtypeStruct((HD, HD, S), f32),
        ),
        in_specs=[vmem, smem] + [vmem] * 7,
        out_specs=(vmem,) * 4,
        scratch_shapes=[
            V((NC,) + mix, bf16),
            V((NC,) + half, bf16),
            V((NC,) + half, bf16),
            V((2, 2) + half, bf16),
            V((2, 2) + half, bf16),
            V((2, 4) + half, bf16),
            V((2, 4) + half, bf16),
            V((2, L // 2, HALF), bf16),
            V((2, L // 2, HALF), bf16),
            V((2,) + half, bf16),
            V((2,) + half, bf16),
            V((NC,) + half, bf16),
            V((NC,) + half, bf16),
            V((NZ,) + mix, bf16),
            V((NZ,) + mix, bf16),
            V((NZ,) + mix, bf16),
            V((NZ,) + mix, bf16),
            V((NZ,) + mix, bf16),
            V((2 * HALF, MODEL), f32),
            V((L, 2 * HALF), f32),
            V((L, 2 * HALF), f32),
            V((2, NC, HH + 1, HD, S), f32),
            V((2, NC, HH + 1, HD, S), f32),
            V((2, NC, HH, HD, S), f32),
            V((2, NC, HH, HD, S), f32),
            V((2, NC, HH + 1, HD, S), f32),
            V((2, NC, HH + 1, HD, S), f32),
            V((2, NC, HH, HD, S), f32),
            V((2, NC, HH, HD, S), f32),
            V((L, S), f32),
            V((L, S), f32),
            V((S, L), f32),
            V((S, L), f32),
            V((S, L), f32),
            V((S, L), f32),
            V((L, L), f32),
        ]
        + [dma((8,))] * 4
        + [dma((32,))] * 8
        + [dma((16,))] * 8
        + [dma((8,))] * 4,
        compiler_params=pltpu.CompilerParams(
            collective_id=0, has_side_effects=True, vmem_limit_bytes=62 * 1024 * 1024
        ),
        cost_estimate=pl.CostEstimate(
            flops=14_000_000_000, bytes_accessed=6_000_000, transcendentals=2_000_000
        ),
        name="mixer",
    )(rates, skip_gain, step_sizes, inner_act, write, read, state_init, out_weight, cotangent)


def solution(mesh):
    placed = (
        P("ctx", "tp"),
        P("ctx", "tp"),
        P("ctx", None, None),
        P("ctx", None, None),
        P("tp"),
        P("tp"),
        P("tp", None, None),
        P("tp", "ctx"),
        P("tp", "ctx"),
    )
    return jax.shard_map(
        local,
        mesh=mesh,
        in_specs=placed,
        out_specs=(P("tp", "ctx"), P("ctx", "tp"), P("tp", "ctx"), P("tp", "ctx", None)),
        check_vma=False,
    )
```

time: 622 us -> 153 us (0.25)
  waiting for transfers between devices: 401 us -> 0 us
  Pallas kernels: 0 us -> 142 us
  blocking collectives: 94.6 us -> 0 us
  matrix products: 50.8 us -> 0 us
  other arithmetic: 41.4 us -> 0 us
  between operations: 14.3 us -> 0.69 us
  local copies, waits for them, and re-layouts: 16.4 us -> 9.92 us
    all_gather x5 -> x0, waiting for transfers between devices: 273 us -> none  [the longest x2 107 us: carried_in(): everything = jax.tree.map(lambda part: lax.all_gather(part, axis), shard)]
    pallas_call x0 -> x1, Pallas kernels: none -> 142 us  [local(): pl.pallas_call(kernel, out_shape=(jax.ShapeDtypeStruct((L, MODEL), bf16),...]
    reduce_scatter x2 -> x0, waiting for transfers between devices: 126 us -> none  [the longest x1 78.1 us: local(): lax.psum_scatter(init_term, 'ctx', scatter_dimension=1, tiled=True)]
    all_to_all x1 -> x0, blocking collectives: 74 us -> none  [local(): lax.all_to_all(cot_all, 'ctx', split_axis=0, concat_axis=1, tiled=True)]
    dot_general x12 -> x0, matrix products: 50.8 us -> none  [the longest x1 11.4 us: local(): jnp.dot(mixer_all, out_weight, preferred_element_type=jnp.float32)]
    select_n x49 -> x0, other arithmetic: 38 us -> none  [the longest x48 38 us: hop(): return jax.tree.map(lambda a, b: jnp.where(reached, a, b), new, before)]
    all_gather x1 -> x0, blocking collectives: 20.6 us -> none  [carried_in(): everything = jax.tree.map(lambda part: lax.all_gather(part, axis), shard)]
    all_to_all x2 -> x0, local copies, waits for them, and re-layouts: 11.9 us -> none  [local(): lax.all_to_all(cot_all, 'ctx', split_axis=0, concat_axis=1, tiled=True)]
  transfers between devices with their start and end apart: 7 -> 0, of which waited for: 7 -> 0; matrix products, arithmetic and copies ran while one was open for 16% -> 0% of each run, Pallas kernels for 0% -> 0%
where the time goes in v1:
time: 153 us; the launch traced here: 152 us
  Pallas kernels  142 us (93%)
  local copies, waits for them, and re-layouts  9.92 us (6%)
    pallas_call x1, Pallas kernels, local(): pl.pallas_call(kernel, out_shape=(jax.ShapeDtypeStruct((L, MODEL), bf16),...  142 us
    unnamed x15, local copies, waits for them, and re-layouts  7.94 us

profile of v1, /device:TPU:2, one launch (start us, length us, event | category | flops | bytes accessed | tf_op | source)
XLA Modules:
  0.0 152.3 jit_solution(14731884604804457558)
XLA Ops:
  0.6 0.0 copy-start.2
  0.7 0.0 copy-start.3
  0.7 0.6 copy-done.3
  1.3 0.5 pad.4.lograte_ref
  1.8 0.0 copy-done.2
  1.8 0.8 copy.16.step_ref
  2.6 1.5 constant_dynamic-slice_fusion
  4.1 0.6 copy.21
  4.7 0.6 copy.22
  5.4 141.7 %mixer.1 = (bf16[256,512]{1,0:T(8,128)(2,1)}, bf16[256,1024]{1,0:T(8,128)(2,1)}, bf16[1024,512]{1,0:T(8,128)(2,1)}, f32[8,8,128]{2,1,0:T(8,128)}) custom-call(f32[1,128]{1,0:T(1,128)} %pad.4.lograte_ref, f32[8]{0:T(128)} %skip_ref.1, f32[256,8]{1,0:T(8,128)} %copy.16.step_ref, bf16[256,1024]{1,0:T(8,128)(2,1)} %x_ref.1, bf16[256,128]{1,0:T(8,128)(2,1)} %bitcast.8, ...), custom_call_target="tpu_custom_call" | custom-call | flops 14000000000 | bytes 6000000 | tf_op jit(solution)/shard_map/mixer/pallas_call | solution.py:608
  147.1 0.0 copy-start
  147.1 1.8 %copy.27 = bf16[256,512]{1,0:T(8,128)(2,1)} copy(bf16[256,512]{1,0:T(8,128)(2,1)} %get-tuple-element.10) | data formatting | bytes 524288
  148.9 1.9 %copy.28 = bf16[256,1024]{1,0:T(8,128)(2,1)} copy(bf16[256,1024]{1,0:T(8,128)(2,1)} %get-tuple-element.11) | data formatting | bytes 1048576
  150.7 0.0 copy-done
  150.7 0.0 copy-start.1
  150.7 1.0 copy.29
  151.7 0.0 copy-done.1
  151.7 0.6 copy.30
Async XLA Ops:
  0.6 1.2 copy-start.2
  0.7 0.7 copy-start.3
  147.1 3.6 %copy-start = (bf16[1024,512]{1,0:T(8,128)(2,1)S(1)}, bf16[1024,512]{1,0:T(8,128)(2,1)}, u32[]{:S(2)}) copy-start(bf16[1024,512]{1,0:T(8,128)(2,1)} %get-tuple-element.12) | copy-start | bytes 3145732
  150.7 1.0 copy-start.1

commit v2 on v1

--- a/solution.py
+++ b/solution.py
@@ -15,6 +15,7 @@
 HALF = 512
 NC = 16
 NZ = 8
+NG = 8
 
 
 def mm(a, b):
@@ -46,12 +47,12 @@
 
 
 def kernel(
-    lograte_ref, skip_ref, step_ref, x_ref, b_ref, c_ref, init_ref, w_ref, cot_ref,
+    lograte_ref, skip_ref, stept_ref, x_ref, in_ref, out_ref, init_ref, w_ref, cot_ref,
     mixed_ref, gi_ref, gw_ref, gs_ref,
     cot_all, pa, pb, r1a, r1b, r2a, r2b, r3a, r3b, r4a, r4b, ma, mb,
     own_mix, xs_mix, xr_mix, zs_mix, zr_mix, gw_acc, ybuf, gbuf,
     sb1, rb1, tb1, ub1, sb2, rb2, tb2, ub2,
-    stp, cum_s, cumt_s, stept_s, bt_s, ct_s, cb_s,
+    stp, cum_s, cumt_s, stept_s, bt_s, ct_s, cb_s, b_ref, c_ref,
     z_s, z_r, c_s, c_r, a1s, a1r, a2s, a2r, a3s, a3r, a4s, a4r,
     rsa_s, rsa_r, rsb_s, rsb_r, aga_s, aga_r, agb_s, agb_r, xm_s, xm_r, zm_s, zm_r,
 ):
@@ -153,21 +154,24 @@
         wait_in(cot_all.at[pblock(d)], c_r.at[index])
 
     lane = lax.broadcasted_iota(jnp.int32, (L, S), 1)
-    stp[...] = jnp.zeros_like(stp)
-    stp[:, 0:HD] = step_ref[...]
-    rate = jnp.exp(lograte_ref[...])
+    head_i = lax.broadcasted_iota(jnp.int32, (HD, L), 0)
+    log_rate = jnp.zeros((HD, L), f32)
+    for h in range(HD):
+        log_rate = jnp.where(head_i == h, lograte_ref[h], log_rate)
     row_i = lax.broadcasted_iota(jnp.int32, (L, L), 0)
     col_i = lax.broadcasted_iota(jnp.int32, (L, L), 1)
-    tri = (row_i >= col_i).astype(f32)
-    cum = lax.dot_general(
-        tri, -stp[...] * rate, (((1,), (0,)), ((), ())),
-        preferred_element_type=f32, precision=lax.Precision.HIGHEST,
-    )
-    cum_s[...] = cum
-    cumt_s[...] = cum.T
-    stept_s[...] = stp[...].T
+    stept_s[...] = jnp.zeros_like(stept_s)
+    stept_s[0:HD, :] = stept_ref[...]
+    cumt_s[...] = jnp.zeros_like(cumt_s)
+    cumt_s[0:HD, :] = lax.dot_general(
+        -stept_ref[...] * jnp.exp(log_rate), (row_i <= col_i).astype(f32),
+        (((1,), (0,)), ((), ())), preferred_element_type=f32, precision=lax.Precision.HIGHEST,
+    )
+    tok_i = lax.broadcasted_iota(jnp.int32, (L, NG * L), 0)
+    tg_i = lax.broadcasted_iota(jnp.int32, (L, NG * L), 1)
+    chosen = (tg_i == tok_i * NG + z).astype(bf16)
+    b_ref[...] = mm(chosen, in_ref[...]).astype(bf16)
     bt_s[...] = b_ref[...].astype(f32).T
-    ct_s[...] = c_ref[...].astype(f32).T
 
     def col(ref, h):
         return jnp.sum(jnp.where(lane == h, ref[...], 0.0), axis=1, keepdims=True)
@@ -210,7 +214,7 @@
             out = []
             for h in range(HH):
                 tb[p, at, h] = states[h]
-                out.append(rb[p, at, HH, h : h + 1, :] * states[h] + rb[p, at, h])
+                out.append(rb1[p, at, HH, h : h + 1, :] * states[h] + rb[p, at, h])
             return tuple(out)
 
         return lax.fori_loop(0, NC, hop, first)
@@ -268,10 +272,13 @@
     zstep(0)
     own_states(1)
     carry_send(1, sb1, rb1, a1s, a1r)
+    c_ref[...] = mm(chosen, out_ref[...]).astype(bf16)
+    ct_s[...] = c_ref[...].astype(f32).T
+    cum_s[...] = cumt_s[...].T
+    stp[...] = stept_s[...].T
     cb_s[...] = mm_bt(c_ref[...], b_ref[...])
+    scan_forward(0)
     own_outputs(0)
-    scan_forward(0)
-    own_outputs(1)
     scan_forward(1)
     zstep(1)
 
@@ -306,8 +313,7 @@
             for i in range(2):
                 send(part.at[blk(far1, q(plus[i]))], r1.at[0, i], i, dev1(n1p))
                 send(part.at[blk(far1, q(minus[i]))], r1.at[1, i], 2 + i, dev1(n1m))
-            for o in minus:
-                send(part.at[blk(n1p, q(o))], r2.at[0, o], 4 + o, dev1(n1p))
+            send(part.at[blk(n1p, q(3))], r2.at[0, 3], 7, dev1(n1p))
             for o in plus:
                 send(part.at[blk(n1m, q(o))], r2.at[1, o], 8 + o, dev1(n1m))
 
@@ -319,6 +325,7 @@
                     j = blk(near, q(o))
                     part[j] = (part[j].astype(f32) + r1[d, i].astype(f32)).astype(bf16)
                     send(part.at[j], r2.at[d, o], 4 + 4 * d + o, dev1(near))
+            send(part.at[blk(n1p, q(0))], r2.at[0, 0], 4, dev1(n1p))
 
         def total(o):
             wait_in(r2.at[0, o], rs.at[4 + o])
@@ -333,7 +340,7 @@
             send(part.at[j, bottom], r3.at[1], 13, dev2(n2m))
 
         def step4():
-            for o, near, rows, d in ((1, n2p, top, 0), (3, n2m, bottom, 1)):
+            for o, near, rows, d in ((3, n2m, bottom, 1), (1, n2p, top, 0)):
                 j = blk(me1, q(o))
                 part[j] = total(o).astype(bf16)
                 wait_in(r3.at[d], rs.at[12 + d])
@@ -468,7 +475,6 @@
             hi, lo = split(ct_s[...] * jnp.exp(row(cumt_s, h)))
             put_piece(sb2, p, i, (mm(hi, ghi) + mm(lo, ghi) + mm(hi, glo)).T)
 
-        put_decay(sb2, p)
         carry_send(p, sb2, rb2, a3s, a3r)
 
     def own_grads(p):
@@ -510,6 +516,7 @@
 
     finish_outputs(0, ma)
     gat_a[0]()
+    own_outputs(1)
     finish_outputs(1, mb)
     gat_b[0]()
     partial_pair(0)
@@ -549,24 +556,22 @@
     pair_send(*late[-1])
     sum_a[1]()
     sum_b[1]()
-    for p in early + late[:1]:
+    for p in early + late:
         pair_weight(*p)
     sum_a[2]()
     sum_b[2]()
-    for p in late[1:]:
-        pair_weight(*p)
+    sum_a[3]()
+    sum_b[3]()
     gw_ref[...] = gw_acc[...].astype(bf16)
     cb_s[...] = mm_bt(b_ref[...], c_ref[...])
-    sum_a[3]()
-    sum_b[3]()
     sum_a[4]()
     own_reach(0)
     sum_b[4]()
     own_reach(1)
     own_grads(0)
     scan_backward(0)
+    scan_backward(1)
     own_grads(1)
-    scan_backward(1)
 
     mixed = zs_mix[z].astype(f32)
     for rel in range(1, NZ):
@@ -595,17 +600,15 @@
 
 def local(inner_act, step_sizes, in_coupling, out_coupling, log_rates, skip_gain, state_init,
           out_weight, cotangent):
-    group = lax.axis_index("tp") // 2
-    write = lax.dynamic_index_in_dim(in_coupling, group, 1, keepdims=False)
-    read = lax.dynamic_index_in_dim(out_coupling, group, 1, keepdims=False)
-    rates = jnp.pad(log_rates.reshape(1, HD), ((0, 0), (0, S - HD)))
+    groups = in_coupling.shape[1]
+    tokens = in_coupling.shape[0]
     vmem = pl.BlockSpec(memory_space=pltpu.VMEM)
     smem = pl.BlockSpec(memory_space=pltpu.SMEM)
     dma = pltpu.SemaphoreType.DMA
     V = pltpu.VMEM
     half = (L, HALF)
     mix = (L, MODEL)
-    return pl.pallas_call(
+    outs = pl.pallas_call(
         kernel,
         out_shape=(
             jax.ShapeDtypeStruct((L, MODEL), bf16),
@@ -613,7 +616,7 @@
             jax.ShapeDtypeStruct((HD * S, MODEL), bf16),
             jax.ShapeDtypeStruct((HD, HD, S), f32),
         ),
-        in_specs=[vmem, smem] + [vmem] * 7,
+        in_specs=[smem, smem] + [vmem] * 7,
         out_specs=(vmem,) * 4,
         scratch_shapes=[
             V((NC,) + mix, bf16),
@@ -641,8 +644,8 @@
             V((2, NC, HH + 1, HD, S), f32),
             V((2, NC, HH, HD, S), f32),
             V((2, NC, HH, HD, S), f32),
-            V((2, NC, HH + 1, HD, S), f32),
-            V((2, NC, HH + 1, HD, S), f32),
+            V((2, NC, HH, HD, S), f32),
+            V((2, NC, HH, HD, S), f32),
             V((2, NC, HH, HD, S), f32),
             V((2, NC, HH, HD, S), f32),
             V((L, S), f32),
@@ -652,6 +655,8 @@
             V((S, L), f32),
             V((S, L), f32),
             V((L, L), f32),
+            V((L, S), bf16),
+            V((L, S), bf16),
         ]
         + [dma((8,))] * 4
         + [dma((32,))] * 8
@@ -664,7 +669,40 @@
             flops=14_000_000_000, bytes_accessed=6_000_000, transcendentals=2_000_000
         ),
         name="mixer",
-    )(rates, skip_gain, step_sizes, inner_act, write, read, state_init, out_weight, cotangent)
+    )(
+        log_rates,
+        skip_gain,
+        step_sizes.T,
+        inner_act,
+        in_coupling.reshape(tokens * groups, S),
+        out_coupling.reshape(tokens * groups, S),
+        state_init,
+        out_weight,
+        cotangent,
+    )
+
+    hbm = pl.BlockSpec(memory_space=pl.ANY)
+    return pl.pallas_call(
+        hand_over,
+        out_shape=tuple(jax.ShapeDtypeStruct(o.shape, o.dtype) for o in outs),
+        in_specs=[hbm] * 4,
+        out_specs=(hbm,) * 4,
+        scratch_shapes=[V(o.shape, o.dtype) for o in outs] + [dma((4,))] * 2,
+        name="hand_over",
+    )(*outs)
+
+
+def hand_over(*refs):
+    held, into, out_of = refs[8:12], refs[12], refs[13]
+    first = [pltpu.make_async_copy(refs[i], held[i], into.at[i]) for i in range(4)]
+    last = [pltpu.make_async_copy(held[i], refs[4 + i], out_of.at[i]) for i in range(4)]
+    for copy in first:
+        copy.start()
+    for i in range(4):
+        first[i].wait()
+        last[i].start()
+    for copy in last:
+        copy.wait()
 
 
 def solution(mesh):

time: 153 us -> 142 us (0.928)
  local copies, waits for them, and re-layouts: 9.92 us -> 0 us
    unnamed x15 -> x0, local copies, waits for them, and re-layouts: 7.94 us -> none
    pallas_call x1, Pallas kernels: 142 us -> 138 us  [local(): pl.pallas_call(kernel, out_shape=(jax.ShapeDtypeStruct((L, MODEL), bf16),...]
    pallas_call x0 -> x1, Pallas kernels: none -> 2.51 us  [local(): pl.pallas_call(hand_over, out_shape=tuple((jax.ShapeDtypeStruct(o.shape,...]
where the time goes in v2:
time: 142 us; the launch traced here: 141 us
  Pallas kernels  141 us (99%)
    pallas_call x1, Pallas kernels, local(): pl.pallas_call(kernel, out_shape=(jax.ShapeDtypeStruct((L, MODEL), bf16),...  138 us

profile of v2, /device:TPU:2, one launch (start us, length us, event | category | flops | bytes accessed | tf_op | source)
XLA Modules:
  0.0 141.4 jit_solution(14776864013994257500)
XLA Ops:
  0.6 138.1 %mixer.1 = (bf16[256,512]{1,0:T(8,128)(2,1)}, bf16[256,1024]{1,0:T(8,128)(2,1)}, bf16[1024,512]{1,0:T(8,128)(2,1)}, f32[8,8,128]{2,1,0:T(8,128)}) custom-call(f32[8]{0:T(128)} %lograte_ref.1, f32[8]{0:T(128)} %skip_ref.1, f32[8,256]{1,0:T(8,128)} %bitcast.5, bf16[256,1024]{1,0:T(8,128)(2,1)} %x_ref.1, bf16[2048,128]{1,0:T(8,128)(2,1)} %bitcast.3, ...), custom_call_target="tpu_custom_call" | custom-call | flops 14000000000 | bytes 6000000 | tf_op jit(solution)/shard_map/mixer/pallas_call | solution.py:611
  138.7 2.5 %hand_over.1 = (bf16[256,512]{1,0:T(8,128)(2,1)}, bf16[256,1024]{1,0:T(8,128)(2,1)}, bf16[1024,512]{1,0:T(8,128)(2,1)}, f32[8,8,128]{2,1,0:T(8,128)}) custom-call(bf16[256,512]{1,0:T(8,128)(2,1)} %get-tuple-element.8.refs_0_, bf16[256,1024]{1,0:T(8,128)(2,1)} %get-tuple-element.9.refs_1_, bf16[1024,512]{1,0:T(8,128)(2,1)} %get-tuple-element.10.refs_2_, ...), custom_call_target="tpu_custom_call" | custom-call | tf_op jit(solution)/shard_map/hand_over/pallas_call | solution.py:685

commit v3 on v2

--- a/solution.py
+++ b/solution.py
@@ -340,17 +340,22 @@
             send(part.at[j, bottom], r3.at[1], 13, dev2(n2m))
 
         def step4():
-            for o, near, rows, d in ((3, n2m, bottom, 1), (1, n2p, top, 0)):
+            order = ((3, n2m, bottom, top, 1), (1, n2p, top, bottom, 0))
+            for o, near, _, free, d in order:
                 j = blk(me1, q(o))
                 part[j] = total(o).astype(bf16)
+                send(part.at[j, free], r4.at[d, free], 14 + d, dev2(near))
+            for o, near, rows, _, d in order:
+                j = blk(me1, q(o))
                 wait_in(r3.at[d], rs.at[12 + d])
                 part[j, rows] = (part[j, rows].astype(f32) + r3[d].astype(f32)).astype(bf16)
-                send(part.at[j], r4.at[d], 14 + d, dev2(near))
+                send(part.at[j, rows], r4.at[d, rows], 16 + d, dev2(near))
 
         def step5():
             mine = total(0)
-            wait_in(r4.at[0], rs.at[14])
-            wait_in(r4.at[1], rs.at[15])
+            for d, rows, free in ((0, top, bottom), (1, bottom, top)):
+                wait_in(r4.at[d, free], rs.at[14 + d])
+                wait_in(r4.at[d, rows], rs.at[16 + d])
             gbuf[:, gcol : gcol + HALF] = mine + r4[0].astype(f32) + r4[1].astype(f32)
 
         return (step1, step2, step3, step4, step5), copies
@@ -660,7 +665,8 @@
         ]
         + [dma((8,))] * 4
         + [dma((32,))] * 8
-        + [dma((16,))] * 8
+        + [dma((18,))] * 4
+        + [dma((16,))] * 4
         + [dma((8,))] * 4,
         compiler_params=pltpu.CompilerParams(
             collective_id=0, has_side_effects=True, vmem_limit_bytes=62 * 1024 * 1024

time: 142 us -> 142 us (level)
  no operation moved by 1% of the time
where the time goes in v3:
time: 142 us; the launch traced here: 141 us
  Pallas kernels  141 us (99%)
    pallas_call x1, Pallas kernels, local(): pl.pallas_call(kernel, out_shape=(jax.ShapeDtypeStruct((L, MODEL), bf16),...  138 us

profile of v3, /device:TPU:2, one launch (start us, length us, event | category | flops | bytes accessed | tf_op | source)
XLA Modules:
  0.0 141.4 jit_solution(9126144418811447155)
XLA Ops:
  0.6 138.1 %mixer.1 = (bf16[256,512]{1,0:T(8,128)(2,1)}, bf16[256,1024]{1,0:T(8,128)(2,1)}, bf16[1024,512]{1,0:T(8,128)(2,1)}, f32[8,8,128]{2,1,0:T(8,128)}) custom-call(f32[8]{0:T(128)} %lograte_ref.1, f32[8]{0:T(128)} %skip_ref.1, f32[8,256]{1,0:T(8,128)} %bitcast.5, bf16[256,1024]{1,0:T(8,128)(2,1)} %x_ref.1, bf16[2048,128]{1,0:T(8,128)(2,1)} %bitcast.3, ...), custom_call_target="tpu_custom_call" | custom-call | flops 14000000000 | bytes 6000000 | tf_op jit(solution)/shard_map/mixer/pallas_call | solution.py:616
  138.8 2.5 %hand_over.1 = (bf16[256,512]{1,0:T(8,128)(2,1)}, bf16[256,1024]{1,0:T(8,128)(2,1)}, bf16[1024,512]{1,0:T(8,128)(2,1)}, f32[8,8,128]{2,1,0:T(8,128)}) custom-call(bf16[256,512]{1,0:T(8,128)(2,1)} %get-tuple-element.8.refs_0_, bf16[256,1024]{1,0:T(8,128)(2,1)} %get-tuple-element.9.refs_1_, bf16[1024,512]{1,0:T(8,128)(2,1)} %get-tuple-element.10.refs_2_, ...), custom_call_target="tpu_custom_call" | custom-call | tf_op jit(solution)/shard_map/hand_over/pallas_call | solution.py:691

commit v4 on v2

--- a/solution.py
+++ b/solution.py
@@ -47,14 +47,14 @@
 
 
 def kernel(
-    lograte_ref, skip_ref, stept_ref, x_ref, in_ref, out_ref, init_ref, w_ref, cot_ref,
+    lograte_ref, skip_ref, stept_ref, x_ref, in_ref, out_hbm, init_hbm, w_hbm, cot_ref,
     mixed_ref, gi_ref, gw_ref, gs_ref,
     cot_all, pa, pb, r1a, r1b, r2a, r2b, r3a, r3b, r4a, r4b, ma, mb,
     own_mix, xs_mix, xr_mix, zs_mix, zr_mix, gw_acc, ybuf, gbuf,
     sb1, rb1, tb1, ub1, sb2, rb2, tb2, ub2,
-    stp, cum_s, cumt_s, stept_s, bt_s, ct_s, cb_s, b_ref, c_ref,
+    stp, cum_s, cumt_s, stept_s, bt_s, ct_s, cb_s, b_ref, c_ref, gw_v, mixed_v, out_ref, init_ref, w_ref,
     z_s, z_r, c_s, c_r, a1s, a1r, a2s, a2r, a3s, a3r, a4s, a4r,
-    rsa_s, rsa_r, rsb_s, rsb_r, aga_s, aga_r, agb_s, agb_r, xm_s, xm_r, zm_s, zm_r,
+    rsa_s, rsa_r, rsb_s, rsb_r, aga_s, aga_r, agb_s, agb_r, xm_s, xm_r, zm_s, zm_r, out_sem, in_sem,
 ):
     ctx = lax.axis_index("ctx")
     tp = lax.axis_index("tp")
@@ -83,6 +83,12 @@
     def wait_out(src, sem):
         rcopy(src, src, sem, sem, other_core).wait_send()
 
+    loads = [
+        pltpu.make_async_copy(src, dst, in_sem.at[i])
+        for i, (src, dst) in enumerate(((out_hbm, out_ref), (init_hbm, init_ref), (w_hbm, w_ref)))
+    ]
+    for load in loads:
+        load.start()
     barrier = pltpu.get_barrier_semaphore()
 
     @pl.loop(1, NC)
@@ -272,6 +278,8 @@
     zstep(0)
     own_states(1)
     carry_send(1, sb1, rb1, a1s, a1r)
+    for load in loads:
+        load.wait()
     c_ref[...] = mm(chosen, out_ref[...]).astype(bf16)
     ct_s[...] = c_ref[...].astype(f32).T
     cum_s[...] = cumt_s[...].T
@@ -562,7 +570,9 @@
     sum_b[2]()
     sum_a[3]()
     sum_b[3]()
-    gw_ref[...] = gw_acc[...].astype(bf16)
+    gw_v[...] = gw_acc[...].astype(bf16)
+    gw_out = pltpu.make_async_copy(gw_v, gw_ref, out_sem.at[0])
+    gw_out.start()
     cb_s[...] = mm_bt(b_ref[...], c_ref[...])
     sum_a[4]()
     own_reach(0)
@@ -577,11 +587,15 @@
     for rel in range(1, NZ):
         wait_in(zr_mix.at[rel], zm_r.at[rel])
         mixed = mixed + zr_mix[rel].astype(f32)
-    mixed_ref[...] = mixed.astype(bf16)
+    mixed_v[...] = mixed.astype(bf16)
+    mixed_out = pltpu.make_async_copy(mixed_v, mixed_ref, out_sem.at[1])
+    mixed_out.start()
 
     finish_grads(0)
     finish_grads(1)
 
+    gw_out.wait()
+    mixed_out.wait()
     for copy in zcopies + copies_a + copies_b + copies_ga + copies_gb:
         copy.wait_send()
     carry_sent(sb1, a1s)
@@ -616,8 +630,8 @@
             jax.ShapeDtypeStruct((HD * S, MODEL), bf16),
             jax.ShapeDtypeStruct((HD, HD, S), f32),
         ),
-        in_specs=[smem, smem] + [vmem] * 7,
-        out_specs=(vmem,) * 4,
+        in_specs=[smem, smem] + [vmem] * 3 + [pl.BlockSpec(memory_space=pl.ANY)] * 3 + [vmem],
+        out_specs=(pl.BlockSpec(memory_space=pl.ANY), vmem, pl.BlockSpec(memory_space=pl.ANY), vmem),
         scratch_shapes=[
             V((NC,) + mix, bf16),
             V((NC,) + half, bf16),
@@ -657,11 +671,17 @@
             V((L, L), f32),
             V((L, S), bf16),
             V((L, S), bf16),
+            V((HD * S, MODEL), bf16),
+            V(mix, bf16),
+            V((NG * L, S), bf16),
+            V((HD, S, S), f32),
+            V((HD * S, MODEL), bf16),
         ]
         + [dma((8,))] * 4
         + [dma((32,))] * 8
         + [dma((16,))] * 8
-        + [dma((8,))] * 4,
+        + [dma((8,))] * 4
+        + [dma((2,)), dma((3,))],
         compiler_params=pltpu.CompilerParams(
             collective_id=0, has_side_effects=True, vmem_limit_bytes=62 * 1024 * 1024
         ),

time: 142 us -> 141 us (level)
  no operation moved by 1% of the time
where the time goes in v4:
time: 141 us; the launch traced here: 140 us
  Pallas kernels  140 us (99%)
    pallas_call x1, Pallas kernels, local(): pl.pallas_call(kernel, out_shape=(jax.ShapeDtypeStruct((L, MODEL), bf16),...  137 us

profile of v4, /device:TPU:2, one launch (start us, length us, event | category | flops | bytes accessed | tf_op | source)
XLA Modules:
  0.0 140.3 jit_solution(12762043623287833472)
XLA Ops:
  0.6 137.0 %mixer.1 = (bf16[256,512]{1,0:T(8,128)(2,1)}, bf16[256,1024]{1,0:T(8,128)(2,1)}, bf16[1024,512]{1,0:T(8,128)(2,1)}, f32[8,8,128]{2,1,0:T(8,128)}) custom-call(f32[8]{0:T(128)} %lograte_ref.1, f32[8]{0:T(128)} %skip_ref.1, f32[8,256]{1,0:T(8,128)} %bitcast.5, bf16[256,1024]{1,0:T(8,128)(2,1)} %x_ref.1, bf16[2048,128]{1,0:T(8,128)(2,1)} %bitcast.3, ...), custom_call_target="tpu_custom_call" | custom-call | flops 14000000000 | bytes 6000000 | tf_op jit(solution)/shard_map/mixer/pallas_call | solution.py:625
  137.6 2.5 %hand_over.1 = (bf16[256,512]{1,0:T(8,128)(2,1)}, bf16[256,1024]{1,0:T(8,128)(2,1)}, bf16[1024,512]{1,0:T(8,128)(2,1)}, f32[8,8,128]{2,1,0:T(8,128)}) custom-call(bf16[256,512]{1,0:T(8,128)(2,1)} %get-tuple-element.8.refs_0_, bf16[256,1024]{1,0:T(8,128)(2,1)} %get-tuple-element.9.refs_1_, bf16[1024,512]{1,0:T(8,128)(2,1)} %get-tuple-element.10.refs_2_, ...), custom_call_target="tpu_custom_call" | custom-call | tf_op jit(solution)/shard_map/hand_over/pallas_call | solution.py:705
